TPU v7x, 512 devices: a whole 4x8x8 slice. The times are simulated.
512 devices in a mesh: gx: 32 (over y_lo, z), gy: 16 (over y_hi, x, core).
Axes of the slice: x: 4, y: 8 (y_hi: 2, y_lo: 4; y = y_hi * 4 + y_lo), z: 8, core: 2. Of those that a mesh axis runs over, the one named last changes fastest.
Arguments:
- features: float32 [131072, 1024], P(('gx', 'gy')), may hold values from -6 to 6
- labels: int32 [512], replicated, may hold values from 0 to 1, as said below
- rounds: int32 [2], replicated, may hold values from 1 to 511, as said below
Outputs:
- feature_grad: float32 [131072, 1024], P(('gx', 'gy'))
Inputs may be any that keep to these rules, and one draw needn't show every extreme that they name: Each of the two values labels some block. `rounds`: 2 different nonzero masks, one of which flips every bit of the block index.
All inputs are finite; a program needn't handle non-finite values.
Results may differ from a plain program's by a relative error of at most 0.0003.
Values sent between devices are 32-bit elements; how exact they have to be, the bound alone decides.
No kernel may reach another device: no remote copies, remote signals or barrier semaphores. Data moves between devices by JAX's collectives and lax.ppermute only.
A program may use at most 64 MiB of HBM per device.

v0:
```python
import jax
import jax.numpy as jnp
from jax import lax
from jax.sharding import PartitionSpec as P


def pair_weight(label_own, label_other, real_rows, fake_rows, loss_scale):
    both_real = loss_scale / (real_rows * (real_rows - 1.0))
    both_fake = loss_scale / (fake_rows * (fake_rows - 1.0))
    mixed = -loss_scale / (real_rows * fake_rows)
    same = label_own == label_other
    return jnp.where(same, jnp.where(label_own == 1, both_real, both_fake), mixed)


def tile_grad(own_rows, partner, weight, skip_diag):
    row_count, feat_width = own_rows.shape
    root_width = jnp.sqrt(jnp.float32(feat_width))
    scores = jnp.dot(own_rows, partner.T, precision=lax.Precision.HIGHEST) / root_width
    coefficient = weight * (6.0 / root_width) * (scores + 1.0) ** 2
    if skip_diag:
        coefficient = jnp.where(jnp.eye(row_count, dtype=bool), jnp.float32(0.0), coefficient)
    return jnp.dot(coefficient, partner, precision=lax.Precision.HIGHEST)


def pick_pieces(spread, offset, peers):
    pieces = spread.reshape(peers, -1, spread.shape[1])
    source_order = jnp.bitwise_xor(jnp.arange(peers, dtype=jnp.int32), offset)
    return jnp.take(pieces, source_order, axis=0)


def fetch_across(block, offset):
    peers = lax.axis_size("gx")
    spread = lax.all_to_all(block, "gx", split_axis=0, concat_axis=0, tiled=True)
    chosen = pick_pieces(spread, offset, peers).reshape(block.shape)
    return lax.all_to_all(chosen, "gx", split_axis=0, concat_axis=0, tiled=True)


def fetch_down(block, offset):
    peers = lax.axis_size("gy")
    spread = lax.all_to_all(block, "gy", split_axis=0, concat_axis=0, tiled=True)
    chosen = pick_pieces(spread, offset, peers).reshape(block.shape)
    return lax.all_to_all(chosen, "gy", split_axis=0, concat_axis=0, tiled=True)


def on_device(features, labels, rounds):
    row_count = features.shape[0]
    down_size = lax.axis_size("gy")
    all_rows = row_count * lax.axis_size("gx") * down_size
    own_block = lax.axis_index("gx") * down_size + lax.axis_index("gy")
    real_rows = jnp.float32(row_count) * jnp.sum(labels).astype(jnp.float32)
    fake_rows = jnp.float32(all_rows) - real_rows
    loss_scale = float(all_rows) * float(all_rows) / 16.0
    label_own = labels[own_block]
    gradient = tile_grad(
        features,
        features,
        pair_weight(label_own, label_own, real_rows, fake_rows, loss_scale),
        True,
    )
    round_total = rounds.shape[0]
    high_parts = [rounds[index] // down_size for index in range(round_total)]
    low_parts = [rounds[index] % down_size for index in range(round_total)]
    crossed = [fetch_across(features, high_parts[index]) for index in range(round_total)]
    partners = [fetch_down(crossed[index], low_parts[index]) for index in range(round_total)]
    for round_index in range(round_total):
        partner_id = jnp.bitwise_xor(own_block, rounds[round_index])
        weight = pair_weight(label_own, labels[partner_id], real_rows, fake_rows, loss_scale)
        gradient = gradient + tile_grad(features, partners[round_index], weight, False)
    return gradient


def solution(mesh):
    in_specs = (P(("gx", "gy"), None), P(), P())
    out_specs = P(("gx", "gy"), None)
    return jax.shard_map(
        on_device, mesh=mesh, in_specs=in_specs, out_specs=out_specs, check_vma=False
    )
```

profile of v0, /device:TPU:73, one launch (start us, length us, event | category | flops | bytes accessed | tf_op | source)
XLA Modules:
  0.0 251.0 jit_solution(12906461820747580402)
XLA Ops:
  0.0 0.0 copy-start.3
  0.0 12.6 %all-to-all-start = ((f32[32,8,1024]{2,1,0:T(8,128)}), f32[32,8,1024]{2,1,0:T(8,128)S(1)}, u32[]{:S(2)}, u32[]{:S(2)}) async-start(f32[32,8,1024]{2,1,0:T(8,128)} %bitcast.22), calls=%async_computation | async-start | bytes 2097152 | tf_op jit(solution)/shard_map/all_to_all | solution.py:33
  12.6 0.0 copy-done.3
  12.6 0.6 fusion.11
  16.1 23.6 %all-to-all-done = f32[32,8,1024]{2,1,0:T(8,128)S(1)} async-done(((f32[32,8,1024]{2,1,0:T(8,128)}), f32[32,8,1024]{2,1,0:T(8,128)S(1)}, u32[]{:S(2)}, u32[]{:S(2)}) %all-to-all-start) | async-done | bytes 1048608 | tf_op jit(solution)/shard_map/all_to_all | solution.py:33
  39.6 0.6 gather_fusion
  40.2 1.1 broadcast_select_fusion.3
  41.3 6.5 %all-to-all-start.1 = ((f32[32,8,1024]{2,1,0:T(8,128)}), f32[32,8,1024]{2,1,0:T(8,128)S(1)}, u32[]{:S(2)}, u32[]{:S(2)}) async-start(f32[32,8,1024]{2,1,0:T(8,128)} %broadcast_select_fusion.3), calls=%async_computation.1 | async-start | bytes 2097152 | tf_op jit(solution)/shard_map/all_to_all | solution.py:35
  50.1 0.6 gather_fusion.2
  50.8 0.1 broadcast_select_fusion.2
  50.9 23.9 %all-to-all-done.1 = f32[32,8,1024]{2,1,0:T(8,128)S(1)} async-done(((f32[32,8,1024]{2,1,0:T(8,128)}), f32[32,8,1024]{2,1,0:T(8,128)S(1)}, u32[]{:S(2)}, u32[]{:S(2)}) %all-to-all-start.1) | async-done | bytes 1048608 | tf_op jit(solution)/shard_map/all_to_all | solution.py:35
  74.8 33.4 %all_to_all.58 = f32[32,8,1024]{2,1,0:T(8,128)} all-to-all(f32[32,8,1024]{2,1,0:T(8,128)S(1)} %broadcast_select_fusion.2), channel_id=1, replica_groups=mesh['gx'=32,'gy'=16] {'gx'}, dimensions={0} | all-to-all | bytes 2097152 | tf_op jit(solution)/shard_map/all_to_all | solution.py:35
  108.2 40.6 %all_to_all.59 = f32[16,16,1024]{2,1,0:T(8,128)S(1)} all-to-all(f32[16,16,1024]{2,1,0:T(8,128)S(1)} %bitcast.27), channel_id=1, replica_groups=mesh['gx'=32,'gy'=16] {'gy'}, dimensions={0} | all-to-all | bytes 2097152 | tf_op jit(solution)/shard_map/all_to_all | solution.py:40
  148.8 3.9 %all-to-all-start.5 = ((f32[16,16,1024]{2,1,0:T(8,128)}), f32[16,16,1024]{2,1,0:T(8,128)S(1)}, u32[]{:S(2)}, u32[]{:S(2)}) async-start(f32[16,16,1024]{2,1,0:T(8,128)} %bitcast.8), calls=%async_computation.5 | async-start | bytes 2097152 | tf_op jit(solution)/shard_map/all_to_all | solution.py:40
  152.7 0.6 gather_fusion.1
  153.3 1.1 broadcast_select_fusion.1
  154.4 27.3 %all-to-all-done.5 = f32[16,16,1024]{2,1,0:T(8,128)S(1)} async-done(((f32[16,16,1024]{2,1,0:T(8,128)}), f32[16,16,1024]{2,1,0:T(8,128)S(1)}, u32[]{:S(2)}, u32[]{:S(2)}) %all-to-all-start.5) | async-done | bytes 1048608 | tf_op jit(solution)/shard_map/all_to_all | solution.py:40
  181.8 4.0 %all-to-all-start.3 = ((f32[16,16,1024]{2,1,0:T(8,128)}), f32[16,16,1024]{2,1,0:T(8,128)S(1)}, u32[]{:S(2)}, u32[]{:S(2)}) async-start(f32[16,16,1024]{2,1,0:T(8,128)} %broadcast_select_fusion.1), calls=%async_computation.3 | async-start | bytes 2097152 | tf_op jit(solution)/shard_map/all_to_all | solution.py:42
  185.8 0.6 gather_fusion.3
  186.4 1.1 broadcast_select_fusion
  187.5 0.0 copy-start
  187.5 27.3 %all-to-all-done.3 = f32[16,16,1024]{2,1,0:T(8,128)S(1)} async-done(((f32[16,16,1024]{2,1,0:T(8,128)}), f32[16,16,1024]{2,1,0:T(8,128)S(1)}, u32[]{:S(2)}, u32[]{:S(2)}) %all-to-all-start.3) | async-done | bytes 1048608 | tf_op jit(solution)/shard_map/all_to_all | solution.py:42
  214.8 4.0 %all-to-all-start.6 = ((f32[16,16,1024]{2,1,0:T(8,128)}), f32[16,16,1024]{2,1,0:T(8,128)S(1)}, u32[]{:S(2)}, u32[]{:S(2)}) async-start(f32[16,16,1024]{2,1,0:T(8,128)} %broadcast_select_fusion), calls=%async_computation.6 | async-start | bytes 2097152 | tf_op jit(solution)/shard_map/all_to_all | solution.py:42
  220.0 0.0 copy-start.2
  220.0 0.7 copy-done.2
  220.7 0.7 reduce_sum.9
  221.4 0.6 fusion.10
  225.8 0.0 copy-done
  225.8 1.0 fusion.9
  226.9 1.0 fusion.12
  227.9 1.0 fusion.5
  229.0 2.0 convolution_add_fusion.1
  231.0 16.8 %all-to-all-done.6 = f32[16,16,1024]{2,1,0:T(8,128)S(1)} async-done(((f32[16,16,1024]{2,1,0:T(8,128)}), f32[16,16,1024]{2,1,0:T(8,128)S(1)}, u32[]{:S(2)}, u32[]{:S(2)}) %all-to-all-start.6) | async-done | bytes 1048608 | tf_op jit(solution)/shard_map/all_to_all | solution.py:42
  247.8 0.0 copy-start.1
  247.8 1.0 fusion.2
  248.8 0.2 copy-done.1
  249.0 2.0 convolution_add_fusion
  (12 shorter events, 0.1 us)
Async XLA Ops:
  0.0 12.6 %copy-start.3 = (s32[2]{0:T(128)S(1)}, s32[2]{0:T(128)}, u32[]{:S(2)}) copy-start(s32[2]{0:T(128)} %param.9) | copy-start | bytes 28
  0.0 39.6 %all-to-all-start = ((f32[32,8,1024]{2,1,0:T(8,128)}), f32[32,8,1024]{2,1,0:T(8,128)S(1)}, u32[]{:S(2)}, u32[]{:S(2)}) async-start(f32[32,8,1024]{2,1,0:T(8,128)} %bitcast.22), calls=%async_computation | async-start | bytes 2097152 | tf_op jit(solution)/shard_map/all_to_all | solution.py:33
  41.3 33.5 %all-to-all-start.1 = ((f32[32,8,1024]{2,1,0:T(8,128)}), f32[32,8,1024]{2,1,0:T(8,128)S(1)}, u32[]{:S(2)}, u32[]{:S(2)}) async-start(f32[32,8,1024]{2,1,0:T(8,128)} %broadcast_select_fusion.3), calls=%async_computation.1 | async-start | bytes 2097152 | tf_op jit(solution)/shard_map/all_to_all | solution.py:35
  148.8 33.0 %all-to-all-start.5 = ((f32[16,16,1024]{2,1,0:T(8,128)}), f32[16,16,1024]{2,1,0:T(8,128)S(1)}, u32[]{:S(2)}, u32[]{:S(2)}) async-start(f32[16,16,1024]{2,1,0:T(8,128)} %bitcast.8), calls=%async_computation.5 | async-start | bytes 2097152 | tf_op jit(solution)/shard_map/all_to_all | solution.py:40
  181.8 33.0 %all-to-all-start.3 = ((f32[16,16,1024]{2,1,0:T(8,128)}), f32[16,16,1024]{2,1,0:T(8,128)S(1)}, u32[]{:S(2)}, u32[]{:S(2)}) async-start(f32[16,16,1024]{2,1,0:T(8,128)} %broadcast_select_fusion.1), calls=%async_computation.3 | async-start | bytes 2097152 | tf_op jit(solution)/shard_map/all_to_all | solution.py:42
  187.5 38.3 %copy-start = (f32[256,1024]{1,0:T(8,128)S(1)}, f32[256,1024]{1,0:T(8,128)}, u32[]{:S(2)}) copy-start(f32[256,1024]{1,0:T(8,128)} %param.7) | copy-start | bytes 3145732
  214.8 33.0 %all-to-all-start.6 = ((f32[16,16,1024]{2,1,0:T(8,128)}), f32[16,16,1024]{2,1,0:T(8,128)S(1)}, u32[]{:S(2)}, u32[]{:S(2)}) async-start(f32[16,16,1024]{2,1,0:T(8,128)} %broadcast_select_fusion), calls=%async_computation.6 | async-start | bytes 2097152 | tf_op jit(solution)/shard_map/all_to_all | solution.py:42
  220.0 0.7 copy-start.2
  247.8 1.2 copy-start.1
where the time goes:
time: 252 us; the launch traced here: 251 us
  waiting for transfers between devices  119 us (47%)
  blocking collectives  74 us (29%)
  starting transfers between devices  30.9 us (12%)
  between operations  10.3 us (4%)
  matrix products  8.17 us (3%)
  local copies, waits for them, and re-layouts  4.52 us (2%)
  other arithmetic  4.26 us (2%)
    all_to_all x2, waiting for transfers between devices, fetch_down(): return lax.all_to_all(chosen, 'gy', split_axis=0, concat_axis=0, tiled=True)  44.1 us
    all_to_all x1, blocking collectives, fetch_down(): lax.all_to_all(block, 'gy', split_axis=0, concat_axis=0, tiled=True)  40.6 us
    all_to_all x1, blocking collectives, fetch_across(): return lax.all_to_all(chosen, 'gx', split_axis=0, concat_axis=0, tiled=True)  33.4 us
    all_to_all x1, waiting for transfers between devices, fetch_down(): lax.all_to_all(block, 'gy', split_axis=0, concat_axis=0, tiled=True)  27.3 us
    all_to_all x1, waiting for transfers between devices, fetch_across(): return lax.all_to_all(chosen, 'gx', split_axis=0, concat_axis=0, tiled=True)  23.9 us
    all_to_all x1, waiting for transfers between devices, fetch_across(): lax.all_to_all(block, 'gx', split_axis=0, concat_axis=0, tiled=True)  23.6 us
    all_to_all x1, starting transfers between devices, fetch_across(): lax.all_to_all(block, 'gx', split_axis=0, concat_axis=0, tiled=True)  12.6 us
    all_to_all x2, starting transfers between devices, fetch_down(): return lax.all_to_all(chosen, 'gy', split_axis=0, concat_axis=0, tiled=True)  7.98 us
  transfers between devices with their start and end apart: 5, of which 5 were waited for; matrix products, arithmetic and copies ran while one was open for 5% of the time, Pallas kernels for 0%

commit v1 on v0

v1 whole, which is shorter than its diff:
```python
import functools
import math

import jax
import jax.numpy as jnp
from jax import lax
from jax.experimental import pallas as pl
from jax.experimental.pallas import tpu as pltpu
from jax.sharding import PartitionSpec as P

AXES = ("gx", "gy")
CORE, X0, X1, Y_HI, Z0, Z1, Z_HI, Y0, Y1 = (1 << place for place in range(9))
LIGHT = (X0, X1, Z0, Y0)
HEAVY = (Z1, Z_HI, Y1, Y_HI)
STRIP = 256


def halves(values):
    high = values.astype(jnp.bfloat16)
    return high, (values - high.astype(jnp.float32)).astype(jnp.bfloat16)


def product(left, right, contract):
    dims = (contract, ((), ()))
    dot = functools.partial(lax.dot_general, dimension_numbers=dims, preferred_element_type=jnp.float32)
    (left_high, left_low), (right_high, right_low) = halves(left), halves(right)
    return dot(left_low, right_high) + dot(left_high, right_low) + dot(left_high, right_high)


def tiles_kernel(blocks, kinds, own_id, rounds, labels, own, *refs):
    partners, out = refs[: len(kinds)], refs[-1]
    base = refs[len(kinds)] if len(refs) > len(kinds) + 1 else None
    row_count, width = own.shape
    marks = labels[...]
    place = lax.broadcasted_iota(jnp.int32, marks.shape, 0) * marks.shape[1] + lax.broadcasted_iota(
        jnp.int32, marks.shape, 1
    )

    def label_at(block):
        return jnp.sum(jnp.where(place == block, marks, 0))

    all_rows = row_count * blocks
    loss_scale = float(all_rows) * float(all_rows) / 16.0
    real_rows = jnp.float32(row_count) * jnp.sum(marks).astype(jnp.float32)
    fake_rows = jnp.float32(all_rows) - real_rows
    block = own_id[0]
    label_own = label_at(block)
    full = blocks - 1
    masks = {"own": 0, "flip": full, "pick": rounds[0] ^ rounds[1] ^ full}
    root_width = math.sqrt(width)
    for index, kind in enumerate(kinds):
        partner = partners[index]
        label_other = label_at(block ^ masks[kind])
        both_real = loss_scale / (real_rows * (real_rows - 1.0))
        both_fake = loss_scale / (fake_rows * (fake_rows - 1.0))
        mixed = -loss_scale / (real_rows * fake_rows)
        weight = jnp.where(label_own == label_other, jnp.where(label_own == 1, both_real, both_fake), mixed)

        def add_scores(step, scores):
            strip = pl.ds(pl.multiple_of(step * STRIP, STRIP), STRIP)
            return scores + product(own[:, strip], partner[:, strip], ((1,), (1,)))

        scores = lax.fori_loop(0, width // STRIP, add_scores, jnp.zeros((row_count, row_count), jnp.float32))
        scores = scores * (1.0 / root_width) + 1.0
        coefficient = (weight * (6.0 / root_width)) * (scores * scores)
        if kind == "own":
            rows = lax.broadcasted_iota(jnp.int32, coefficient.shape, 0)
            columns = lax.broadcasted_iota(jnp.int32, coefficient.shape, 1)
            coefficient = jnp.where(rows == columns, 0.0, coefficient)
        before = base if index == 0 else out

        def add_gradient(step, carry):
            strip = pl.ds(pl.multiple_of(step * STRIP, STRIP), STRIP)
            part = product(coefficient, partner[:, strip], ((1,), (0,)))
            out[:, strip] = part if before is None else before[:, strip] + part
            return carry

        lax.fori_loop(0, width // STRIP, add_gradient, 0)


def add_tiles(blocks, kinds, own_id, rounds, labels, own, partners, base=None):
    row_count, width = own.shape
    scalars = [pl.BlockSpec(memory_space=pltpu.SMEM)] * 2
    arrays = [labels, own, *partners] + ([] if base is None else [base])
    flops = 4 * len(kinds) * row_count * row_count * width
    return pl.pallas_call(
        functools.partial(tiles_kernel, blocks, kinds),
        out_shape=jax.ShapeDtypeStruct(own.shape, jnp.float32),
        in_specs=scalars + [pl.BlockSpec(memory_space=pltpu.VMEM)] * len(arrays),
        out_specs=pl.BlockSpec(memory_space=pltpu.VMEM),
        compiler_params=pltpu.CompilerParams(vmem_limit_bytes=32 << 20),
        cost_estimate=pl.CostEstimate(
            flops=3 * flops, bytes_accessed=4 * row_count * width * len(arrays), transcendentals=0
        ),
    )(own_id, rounds, *arrays)


def flip(block, mask):
    count = lax.axis_size("gx") * lax.axis_size("gy")
    return lax.ppermute(block, AXES, [(source, source ^ mask) for source in range(count)])


def flip_by(block, mask, bits):
    choice = jnp.int32(0)
    for place, bit in enumerate(bits):
        choice = choice | (((mask & bit) != 0).astype(jnp.int32) << place)
    masks = [sum(bit for place, bit in enumerate(bits) if pick >> place & 1) for pick in range(1 << len(bits))]
    branches = [(lambda rows, m=m: flip(rows, m) if m else rows) for m in masks]
    return lax.switch(choice, branches, block)


def on_device(features, labels, rounds):
    blocks = lax.axis_size("gx") * lax.axis_size("gy")
    full = blocks - 1
    own_block = lax.axis_index("gx") * lax.axis_size("gy") + lax.axis_index("gy")
    own_id = own_block.astype(jnp.int32).reshape(1)
    labels = labels.reshape(-1, 128)
    mask = rounds[0] ^ rounds[1] ^ full
    far = flip(features, full)
    sibling = flip(features, CORE)
    gradient = add_tiles(blocks, ("own",), own_id, rounds, labels, features, (features,))
    near = jnp.where((mask & CORE) != 0, sibling, features)
    near = flip_by(near, mask, LIGHT)
    near = flip_by(near, mask, HEAVY)
    return add_tiles(blocks, ("flip", "pick"), own_id, rounds, labels, features, (far, near), gradient)


def solution(mesh):
    in_specs = (P(("gx", "gy"), None), P(), P())
    out_specs = P(("gx", "gy"), None)
    return jax.shard_map(
        on_device, mesh=mesh, in_specs=in_specs, out_specs=out_specs, check_vma=False
    )
```

time: 252 us -> 188 us (0.75)
  the two profiles are of different devices: /device:TPU:73 before, /device:TPU:30 now
where the time goes in v1:
time: 188 us; the launch traced here: 187 us
  waiting for transfers between devices  145 us (77%)
  starting transfers between devices  25.2 us (13%)
  Pallas kernels  10.7 us (6%)
  local copies, waits for them, and re-layouts  4.43 us (2%)
    ppermute x4, waiting for transfers between devices, flip(): lax.ppermute(block, AXES, [(source, source ^ mask) for source in range(co...  145 us
    ppermute x4, starting transfers between devices, flip(): lax.ppermute(block, AXES, [(source, source ^ mask) for source in range(co...  25.2 us
    pallas_call x2, Pallas kernels, add_tiles(): pl.pallas_call(functools.partial(tiles_kernel, blocks, kinds), out_shape=...  10.7 us
  transfers between devices with their start and end apart: 4, of which 2 were waited for; matrix products, arithmetic and copies ran while one was open for 2% of the time, Pallas kernels for 2%

profile of v1, /device:TPU:30, one launch (start us, length us, event | category | flops | bytes accessed | tf_op | source)
XLA Modules:
  0.0 187.2 jit_solution(7132979360952358529)
XLA Ops:
  0.0 0.0 copy-start.2
  0.0 2.0 %collective-permute-start.31 = (f32[256,1024]{1,0:T(8,128)}, f32[256,1024]{1,0:T(8,128)S(1)}, u32[]{:S(2)}, u32[]{:S(2)}) collective-permute-start(f32[256,1024]{1,0:T(8,128)} %own.3), channel_id=1, source_target_pairs={{0,1},{1,0},{2,3},{3,2},{4,5},{5,4},{6,7},{7,6},{8,9},{9,8},{10,11... | collective-permute-start | bytes 3145736 | tf_op jit(solution)/shard_map/ppermute | solution.py:100
  2.1 13.2 %collective-permute-start.30 = (f32[256,1024]{1,0:T(8,128)}, f32[256,1024]{1,0:T(8,128)S(1)}, u32[]{:S(2)}, u32[]{:S(2)}) collective-permute-start(f32[256,1024]{1,0:T(8,128)} %own.3), channel_id=1, source_target_pairs={{0,511},{1,510},{2,509},{3,508},{4,507},{5,506},{6,505},{7,504},{8... | collective-permute-start | bytes 3145736 | tf_op jit(solution)/shard_map/ppermute | solution.py:100
  15.3 0.0 copy-done.2
  15.3 0.6 fusion
  17.1 0.0 copy-start.3
  17.1 0.7 copy-done.3
  17.8 0.0 copy-start
  17.8 1.2 copy-done
  19.0 3.2 %shard_map.37.refs_2_ = f32[256,1024]{1,0:T(8,128)S(1)} custom-call(s32[1]{0:T(128)} %bitcast.own_id, s32[2]{0:T(128)S(1)} %copy-done.2, s32[4,128]{1,0:T(4,128)S(1)} %bitcast.5, f32[256,1024]{1,0:T(8,128)S(1)} %copy-done, f32[256,1024]{1,0:T(8,128)S(1)} %copy-done), custom_call_target="tpu_custom_call" | custom-call | flops 805306368 | bytes 3145728 | tf_op jit(solution)/shard_map/pallas_call | solution.py:86
  22.2 0.0 collective-permute-done.31
  22.2 1.1 broadcast_select_fusion
  23.4 63.6 %conditional.2 = (f32[256,1024]{1,0:T(8,128)}) conditional(s32[]{:T(128)} %bitcast.3, f32[256,1024]{1,0:T(8,128)} %broadcast_select_fusion, f32[256,1024]{1,0:T(8,128)} %broadcast_select_fusion, f32[256,1024]{1,0:T(8,128)} %broadcast_select_fusion, f32[256,1024]{1,0:T(8,128)} %broadcast_select_fusion, ...), branch_computations={%region_0.1_spmd, %region_1.2_spmd, %region_2.3_spmd, %region_3.4_... | conditional | bytes 6291504 | solution.py:109
  23.4 6.2 %collective-permute-start.13 = (f32[256,1024]{1,0:T(8,128)}, f32[256,1024]{1,0:T(8,128)S(1)}, u32[]{:S(2)}, u32[]{:S(2)}) collective-permute-start(f32[256,1024]{1,0:T(8,128)} %param.14), channel_id=1, source_target_pairs={{0,148},{1,149},{2,150},{3,151},{4,144},{5,145},{6,146},{7,147},{8... | collective-permute-start | bytes 3145736 | tf_op jit(solution)/shard_map/cond/branch_14_fun/ppermute | solution.py:100
  29.6 56.4 %collective-permute-done.13 = f32[256,1024]{1,0:T(8,128)S(1)} collective-permute-done((f32[256,1024]{1,0:T(8,128)}, f32[256,1024]{1,0:T(8,128)S(1)}, u32[]{:S(2)}, u32[]{:S(2)}) %collective-permute-start.13) | collective-permute-done | bytes 1048608 | tf_op jit(solution)/shard_map/cond/branch_14_fun/ppermute | solution.py:100
  86.0 1.0 copy.18
  87.0 0.0 copy-start.1
  87.0 92.8 %conditional.3 = (f32[256,1024]{1,0:T(8,128)}) conditional(s32[]{:T(128)} %bitcast.2, f32[256,1024]{1,0:T(8,128)} %get-tuple-element.73, f32[256,1024]{1,0:T(8,128)} %get-tuple-element.73, f32[256,1024]{1,0:T(8,128)} %get-tuple-element.73, f32[256,1024]{1,0:T(8,128)} %get-tuple-element.73, ...), branch_computations={%region_16.17_spmd, %region_17.18_spmd, %region_18.19_spmd, %regio... | conditional | bytes 6291504 | solution.py:109
  87.0 3.7 %collective-permute-start.23 = (f32[256,1024]{1,0:T(8,128)}, f32[256,1024]{1,0:T(8,128)S(1)}, u32[]{:S(2)}, u32[]{:S(2)}) collective-permute-start(f32[256,1024]{1,0:T(8,128)} %param.25), channel_id=1, source_target_pairs={{0,40},{1,41},{2,42},{3,43},{4,44},{5,45},{6,46},{7,47},{8,32},{9,... | collective-permute-start | bytes 3145736 | tf_op jit(solution)/shard_map/cond/branch_9_fun/ppermute | solution.py:100
  90.7 88.1 %collective-permute-done.23 = f32[256,1024]{1,0:T(8,128)S(1)} collective-permute-done((f32[256,1024]{1,0:T(8,128)}, f32[256,1024]{1,0:T(8,128)S(1)}, u32[]{:S(2)}, u32[]{:S(2)}) %collective-permute-start.23) | collective-permute-done | bytes 1048608 | tf_op jit(solution)/shard_map/cond/branch_9_fun/ppermute | solution.py:100
  178.8 1.0 copy.29
  179.8 0.0 collective-permute-done.30.refs_0_
  179.8 0.0 copy-done.1
  179.8 7.5 %shard_map.38 = f32[256,1024]{1,0:T(8,128)} custom-call(s32[1]{0:T(128)} %bitcast.own_id, s32[2]{0:T(128)S(1)} %copy-done.2, s32[4,128]{1,0:T(4,128)S(1)} %bitcast.6, f32[256,1024]{1,0:T(8,128)S(1)} %copy-done.1, f32[256,1024]{1,0:T(8,128)S(1)} %collective-permute-done.30.refs_0_, f32[256,1024]{1,0:T(8,128)} %get-tuple-element.74.refs_1_, ...), custom_call_target="tpu_custom_call" | custom-call | flops 1610612736 | bytes 5242880 | tf_op jit(solution)/shard_map/pallas_call | solution.py:86
Async XLA Ops:
  0.0 15.3 %copy-start.2 = (s32[2]{0:T(128)S(1)}, s32[2]{0:T(128)}, u32[]{:S(2)}) copy-start(s32[2]{0:T(128)} %rounds.3) | copy-start | bytes 28
  0.0 22.2 %collective-permute-start.31 = (f32[256,1024]{1,0:T(8,128)}, f32[256,1024]{1,0:T(8,128)S(1)}, u32[]{:S(2)}, u32[]{:S(2)}) collective-permute-start(f32[256,1024]{1,0:T(8,128)} %own.3), channel_id=1, source_target_pairs={{0,1},{1,0},{2,3},{3,2},{4,5},{5,4},{6,7},{7,6},{8,9},{9,8},{10,11... | collective-permute-start | bytes 3145736 | tf_op jit(solution)/shard_map/ppermute | solution.py:100
  2.1 177.7 %collective-permute-start.30 = (f32[256,1024]{1,0:T(8,128)}, f32[256,1024]{1,0:T(8,128)S(1)}, u32[]{:S(2)}, u32[]{:S(2)}) collective-permute-start(f32[256,1024]{1,0:T(8,128)} %own.3), channel_id=1, source_target_pairs={{0,511},{1,510},{2,509},{3,508},{4,507},{5,506},{6,505},{7,504},{8... | collective-permute-start | bytes 3145736 | tf_op jit(solution)/shard_map/ppermute | solution.py:100
  17.1 0.7 copy-start.3
  17.8 1.2 copy-start
  23.4 62.6 %collective-permute-start.13 = (f32[256,1024]{1,0:T(8,128)}, f32[256,1024]{1,0:T(8,128)S(1)}, u32[]{:S(2)}, u32[]{:S(2)}) collective-permute-start(f32[256,1024]{1,0:T(8,128)} %param.14), channel_id=1, source_target_pairs={{0,148},{1,149},{2,150},{3,151},{4,144},{5,145},{6,146},{7,147},{8... | collective-permute-start | bytes 3145736 | tf_op jit(solution)/shard_map/cond/branch_14_fun/ppermute | solution.py:100
  87.0 92.8 %copy-start.1 = (f32[256,1024]{1,0:T(8,128)S(1)}, f32[256,1024]{1,0:T(8,128)}, u32[]{:S(2)}) copy-start(f32[256,1024]{1,0:T(8,128)} %own.3) | copy-start | bytes 3145732
  87.0 91.8 %collective-permute-start.23 = (f32[256,1024]{1,0:T(8,128)}, f32[256,1024]{1,0:T(8,128)S(1)}, u32[]{:S(2)}, u32[]{:S(2)}) collective-permute-start(f32[256,1024]{1,0:T(8,128)} %param.25), channel_id=1, source_target_pairs={{0,40},{1,41},{2,42},{3,43},{4,44},{5,45},{6,46},{7,47},{8,32},{9,... | collective-permute-start | bytes 3145736 | tf_op jit(solution)/shard_map/cond/branch_9_fun/ppermute | solution.py:100

commit v2 on v1

v2 whole, which is shorter than its diff:
```python
import functools
import math

import jax
import jax.numpy as jnp
from jax import lax
from jax.experimental import pallas as pl
from jax.experimental.pallas import tpu as pltpu
from jax.sharding import PartitionSpec as P

AXES = ("gx", "gy")
CORE, X0, X1, Y_HI, Z0, Z1, Z_HI, Y0, Y1 = (1 << place for place in range(9))
def halves(values):
    high = values.astype(jnp.bfloat16)
    return high, (values - high.astype(jnp.float32)).astype(jnp.bfloat16)


def dot(left, right, contract):
    return lax.dot_general(left, right, (contract, ((), ())), preferred_element_type=jnp.float32)


def product(left_pair, right_high, right_low, contract):
    rows = left_pair.shape[0] // 2
    both = dot(left_pair, right_high, contract)
    return (both[rows:] + dot(left_pair[:rows], right_low, contract)) + both[:rows]


def tiles_kernel(blocks, kinds, parts, own_id, rounds, labels, own, *refs):
    partners, rest = refs[: sum(parts)], refs[sum(parts) :]
    base = rest[0] if len(rest) == 6 else None
    out, own_pair, high, low, landing = rest[-5:]
    row_count, width = own.shape
    marks = labels[...]
    place = lax.broadcasted_iota(jnp.int32, marks.shape, 0) * marks.shape[1] + lax.broadcasted_iota(
        jnp.int32, marks.shape, 1
    )

    def label_at(block):
        return jnp.sum(jnp.where(place == block, marks, 0))

    all_rows = row_count * blocks
    loss_scale = float(all_rows) * float(all_rows) / 16.0
    real_rows = jnp.float32(row_count) * jnp.sum(marks).astype(jnp.float32)
    fake_rows = jnp.float32(all_rows) - real_rows
    both_real = loss_scale / (real_rows * (real_rows - 1.0))
    both_fake = loss_scale / (fake_rows * (fake_rows - 1.0))
    mixed = -loss_scale / (real_rows * fake_rows)
    block = own_id[0]
    label_own = label_at(block)
    full = blocks - 1
    masks = {"own": 0, "flip": full, "pick": rounds[0] ^ rounds[1] ^ full}
    root_width = math.sqrt(width)
    own_pair[:row_count, :], own_pair[row_count:, :] = halves(own[...])
    total = None if base is None else base[...]
    first = 0
    for kind, count in zip(kinds, parts):
        rows = 0
        for piece in partners[first : first + count]:
            here = slice(rows, rows + piece.shape[0])
            high[here, :], low[here, :] = halves(piece[...])
            rows += piece.shape[0]
        first += count
        weight = jnp.where(
            label_own == label_at(block ^ masks[kind]), jnp.where(label_own == 1, both_real, both_fake), mixed
        )
        right_high, right_low = high[:rows, :], low[:rows, :]
        scores = product(own_pair[...], right_high, right_low, ((1,), (1,))) * (1.0 / root_width) + 1.0
        coefficient = (weight * (6.0 / root_width)) * (scores * scores)
        if kind == "own":
            down = lax.broadcasted_iota(jnp.int32, coefficient.shape, 0)
            across = lax.broadcasted_iota(jnp.int32, coefficient.shape, 1)
            coefficient = jnp.where(down == across, 0.0, coefficient)
        pair = jnp.concatenate(halves(coefficient), axis=0)
        part = product(pair, right_high, right_low, ((1,), (0,)))
        total = part if total is None else total + part
        out[...] = total
        total = out[...]


def add_tiles(blocks, tiles, own_id, rounds, labels, own, base=None):
    row_count, width = own.shape
    scalar, held = pl.BlockSpec(memory_space=pltpu.SMEM), pl.BlockSpec(memory_space=pltpu.VMEM)
    kinds, parts = tuple(kind for kind, _ in tiles), tuple(len(pieces) for _, pieces in tiles)
    arrays = [labels, own] + [piece for _, pieces in tiles for piece in pieces] + ([] if base is None else [base])
    flops = 4 * len(kinds) * row_count * row_count * width
    return pl.pallas_call(
        functools.partial(tiles_kernel, blocks, kinds, parts),
        out_shape=jax.ShapeDtypeStruct(own.shape, jnp.float32),
        in_specs=[scalar, scalar] + [held] * len(arrays),
        out_specs=held,
        scratch_shapes=[
            pltpu.VMEM((2 * row_count, width), jnp.bfloat16),
            pltpu.VMEM((row_count, width), jnp.bfloat16),
            pltpu.VMEM((row_count, width), jnp.bfloat16),
            pltpu.VMEM((8, 128), jnp.float32),
        ],
        compiler_params=pltpu.CompilerParams(vmem_limit_bytes=32 << 20),
        cost_estimate=pl.CostEstimate(
            flops=3 * flops, bytes_accessed=4 * row_count * width * len(arrays), transcendentals=0
        ),
    )(own_id, rounds, *arrays)


def flip(block, mask):
    count = lax.axis_size("gx") * lax.axis_size("gy")
    return lax.ppermute(block, AXES, [(source, source ^ mask) for source in range(count)]) if mask else block


def subsets(bits):
    return [sum(bit for place, bit in enumerate(bits) if pick >> place & 1) for pick in range(1 << len(bits))]


def packed(flags):
    return sum(flag.astype(jnp.int32) << place for place, flag in enumerate(flags))


def on_device(features, labels, rounds):
    blocks = lax.axis_size("gx") * lax.axis_size("gy")
    full = blocks - 1
    own_block = lax.axis_index("gx") * lax.axis_size("gy") + lax.axis_index("gy")
    own_id = own_block.astype(jnp.int32).reshape(1)
    labels = labels.reshape(-1, 128)
    mask = rounds[0] ^ rounds[1] ^ full
    bit = {place: (mask & place) != 0 for place in (CORE, X0, X1, Y_HI, Z0, Z1, Z_HI, Y0, Y1)}
    half = features.shape[0] // 2
    top, bottom = features[:half], features[half:]

    inner = packed([bit[Y0] ^ bit[Y_HI], bit[Y1] ^ bit[Y_HI], bit[Z0] ^ bit[Z_HI], bit[Z1] ^ bit[Z_HI]])
    inner_moves = [functools.partial(flip, mask=move) for move in subsets((Y0, Y1, Z0, Z1))]

    far_bottom = flip(bottom, full)
    top_moved = lax.switch(inner, inner_moves, top)
    top_later, top_moved = lax.optimization_barrier((top, top_moved))
    far_top = flip(top_later, full)
    bottom_moved = lax.switch(inner, inner_moves, far_bottom)

    cross = bit[Y_HI]
    stays, crosses = jnp.where(cross, bottom_moved, top_moved), jnp.where(cross, top_moved, bottom_moved)
    along = (X0, X1, Z0 | Z1 | Z_HI)
    outer = packed([bit[place] ^ cross for place in (X0, X1, Z_HI)])
    rest = Y0 | Y1 | Y_HI | sum(along)
    outer_moves = [
        (lambda pair, move=move: (flip(pair[0], move), flip(pair[1], move ^ rest))) for move in subsets(along)
    ]
    stays, crosses = lax.switch(outer, outer_moves, (stays, crosses))

    swap = bit[CORE] ^ cross
    ready, sibling = jnp.where(swap, crosses, stays), jnp.where(swap, stays, crosses)
    swapped = flip(sibling, CORE)
    tiles = [("own", (features,)), ("flip", (far_top, far_bottom)), ("pick", (ready,))]
    gradient = add_tiles(blocks, tiles, own_id, rounds, labels, features)
    return add_tiles(blocks, [("pick", (swapped,))], own_id, rounds, labels, features, gradient)


def solution(mesh):
    in_specs = (P(("gx", "gy"), None), P(), P())
    out_specs = P(("gx", "gy"), None)
    return jax.shard_map(
        on_device, mesh=mesh, in_specs=in_specs, out_specs=out_specs, check_vma=False
    )
```

time: 188 us -> 132 us (0.70)
  the two profiles are of different devices: /device:TPU:30 before, /device:TPU:1 now
where the time goes in v2:
time: 132 us; the launch traced here: 131 us
  waiting for transfers between devices  70.2 us (53%)
  starting transfers between devices  45.8 us (35%)
  Pallas kernels  8.01 us (6%)
  other arithmetic  3.27 us (2%)
  local copies, waits for them, and re-layouts  2.57 us (2%)
  between operations  1.43 us (1%)
    ppermute x7, waiting for transfers between devices, flip(): lax.ppermute(block, AXES, [(source, source ^ mask) for source in range(co...  70.2 us
    ppermute x7, starting transfers between devices, flip(): lax.ppermute(block, AXES, [(source, source ^ mask) for source in range(co...  45.8 us
    pallas_call x2, Pallas kernels, add_tiles(): pl.pallas_call(functools.partial(tiles_kernel, blocks, kinds, parts), out...  8.01 us
  transfers between devices with their start and end apart: 7, of which 4 were waited for; matrix products, arithmetic and copies ran while one was open for 3% of the time, Pallas kernels for 4%

profile of v2, /device:TPU:1, one launch (start us, length us, event | category | flops | bytes accessed | tf_op | source)
XLA Modules:
  0.0 131.4 jit_solution(507686188595724538)
XLA Ops:
  0.0 1.3 fusion
  1.3 0.0 copy-start.1
  1.3 17.2 %collective-permute-start.45 = (f32[128,1024]{1,0:T(8,128)S(1)}, f32[128,1024]{1,0:T(8,128)}, u32[]{:S(2)}, u32[]{:S(2)}) collective-permute-start(f32[128,1024]{1,0:T(8,128)S(1)} %get-tuple-element.131), channel_id=1, source_target_pairs={{0,511},{1,510},{2,509},{3,508},{4,507},{5,506},{6,505},{7,504},{8... | collective-permute-start | bytes 1572872 | tf_op jit(solution)/shard_map/ppermute | solution.py:106
  18.5 0.0 copy-done.1
  18.5 0.6 fusion.1
  20.3 27.3 %conditional.3 = (f32[128,1024]{1,0:T(8,128)}) conditional(s32[]{:T(128)} %clamp.8, f32[128,1024]{1,0:T(8,128)S(1)} %get-tuple-element.126, f32[128,1024]{1,0:T(8,128)S(1)} %get-tuple-element.126, f32[128,1024]{1,0:T(8,128)S(1)} %get-tuple-element.126, f32[128,1024]{1,0:T(8,128)S(1)} %get-tuple-element.126, ...), branch_computations={%region_0.0_spmd, %region_1.0_spmd, %region_2.0_spmd, %region_3.0_... | conditional | bytes 2097200 | solution.py:132
  20.4 5.4 %collective-permute-start.6 = (f32[128,1024]{1,0:T(8,128)S(1)}, f32[128,1024]{1,0:T(8,128)}, u32[]{:S(2)}, u32[]{:S(2)}) collective-permute-start(f32[128,1024]{1,0:T(8,128)S(1)} %param.7), channel_id=1, source_target_pairs={{0,400},{1,401},{2,402},{3,403},{4,404},{5,405},{6,406},{7,407},{8... | collective-permute-start | bytes 1572872 | tf_op jit(solution)/shard_map/cond/branch_7_fun/ppermute | solution.py:106
  25.8 21.8 %collective-permute-done.6 = f32[128,1024]{1,0:T(8,128)} collective-permute-done((f32[128,1024]{1,0:T(8,128)S(1)}, f32[128,1024]{1,0:T(8,128)}, u32[]{:S(2)}, u32[]{:S(2)}) %collective-permute-start.6) | collective-permute-done | bytes 524320 | tf_op jit(solution)/shard_map/cond/branch_7_fun/ppermute | solution.py:106
  47.6 1.9 %collective-permute-start.47 = (f32[128,1024]{1,0:T(8,128)S(1)}, f32[128,1024]{1,0:T(8,128)S(1)}, u32[]{:S(2)}, u32[]{:S(2)}) collective-permute-start(f32[128,1024]{1,0:T(8,128)S(1)} %get-tuple-element.126), channel_id=1, source_target_pairs={{0,511},{1,510},{2,509},{3,508},{4,507},{5,506},{6,505},{7,504},{8... | collective-permute-start | bytes 1572872 | tf_op jit(solution)/shard_map/ppermute | solution.py:106
  49.6 0.0 collective-permute-done.45.refs_2_
  49.6 30.0 %conditional.4 = (f32[128,1024]{1,0:T(8,128)}) conditional(s32[]{:T(128)} %clamp.8, f32[128,1024]{1,0:T(8,128)} %collective-permute-done.45.refs_2_, f32[128,1024]{1,0:T(8,128)} %collective-permute-done.45.refs_2_, f32[128,1024]{1,0:T(8,128)} %collective-permute-done.45.refs_2_, ...), branch_computations={%region_16.0_spmd, %region_17.0_spmd, %region_18.0_spmd, %region_1... | conditional | bytes 2097200 | solution.py:135
  49.6 6.1 %collective-permute-start.21 = (f32[128,1024]{1,0:T(8,128)}, f32[128,1024]{1,0:T(8,128)}, u32[]{:S(2)}, u32[]{:S(2)}) collective-permute-start(f32[128,1024]{1,0:T(8,128)} %param.23), channel_id=1, source_target_pairs={{0,400},{1,401},{2,402},{3,403},{4,404},{5,405},{6,406},{7,407},{8... | collective-permute-start | bytes 1572872 | tf_op jit(solution)/shard_map/cond/branch_7_fun/ppermute | solution.py:106
  55.7 23.9 %collective-permute-done.21 = f32[128,1024]{1,0:T(8,128)} collective-permute-done((f32[128,1024]{1,0:T(8,128)}, f32[128,1024]{1,0:T(8,128)}, u32[]{:S(2)}, u32[]{:S(2)}) %collective-permute-start.21) | collective-permute-done | bytes 524320 | tf_op jit(solution)/shard_map/cond/branch_7_fun/ppermute | solution.py:106
  79.6 1.3 broadcast_select_fusion
  80.9 36.0 %conditional.5 = (f32[128,1024]{1,0:T(8,128)S(1)}, f32[128,1024]{1,0:T(8,128)}) conditional(s32[]{:T(128)} %clamp.7, (f32[128,1024]{1,0:T(8,128)S(1)}, f32[128,1024]{1,0:T(8,128)S(1)}) %tuple.135, (f32[128,1024]{1,0:T(8,128)S(1)}, f32[128,1024]{1,0:T(8,128)S(1)}) %broadcast_select_fusion, (f32[128,1024]{1,0:T(8,128)S(1)}, ...), branch_computations={%region_32.33_spmd, %region_33.34_spmd, %region_34.35_spmd, %regio... | conditional | bytes 5242976 | solution.py:145
  81.0 6.9 %collective-permute-start.37 = (f32[128,1024]{1,0:T(8,128)S(1)}, f32[128,1024]{1,0:T(8,128)S(1)}, u32[]{:S(2)}, u32[]{:S(2)}) collective-permute-start(f32[128,1024]{1,0:T(8,128)S(1)} %get-tuple-element.111), channel_id=1, source_target_pairs={{0,112},{1,113},{2,114},{3,115},{4,116},{5,117},{6,118},{7,119},{8... | collective-permute-start | bytes 1572872 | tf_op jit(solution)/shard_map/cond/branch_4_fun/ppermute | solution.py:106
  87.9 4.6 %collective-permute-start.38 = (f32[128,1024]{1,0:T(8,128)S(1)}, f32[128,1024]{1,0:T(8,128)}, u32[]{:S(2)}, u32[]{:S(2)}) collective-permute-start(f32[128,1024]{1,0:T(8,128)S(1)} %get-tuple-element.112), channel_id=1, source_target_pairs={{0,398},{1,399},{2,396},{3,397},{4,394},{5,395},{6,392},{7,393},{8... | collective-permute-start | bytes 1572872 | tf_op jit(solution)/shard_map/cond/branch_4_fun/ppermute | solution.py:106
  92.4 19.1 %collective-permute-done.37 = f32[128,1024]{1,0:T(8,128)S(1)} collective-permute-done((f32[128,1024]{1,0:T(8,128)S(1)}, f32[128,1024]{1,0:T(8,128)S(1)}, u32[]{:S(2)}, u32[]{:S(2)}) %collective-permute-start.37) | collective-permute-done | bytes 524320 | tf_op jit(solution)/shard_map/cond/branch_4_fun/ppermute | solution.py:106
  111.6 5.3 %collective-permute-done.38 = f32[128,1024]{1,0:T(8,128)} collective-permute-done((f32[128,1024]{1,0:T(8,128)S(1)}, f32[128,1024]{1,0:T(8,128)}, u32[]{:S(2)}, u32[]{:S(2)}) %collective-permute-start.38) | collective-permute-done | bytes 524320 | tf_op jit(solution)/shard_map/cond/branch_4_fun/ppermute | solution.py:106
  116.9 0.0 copy-start
  116.9 2.0 %broadcast_select_fusion.2 = (f32[128,1024]{1,0:T(8,128)S(1)}, f32[128,1024]{1,0:T(8,128)}) fusion(f32[128,1024]{1,0:T(8,128)} %get-tuple-element.125, f32[128,1024]{1,0:T(8,128)S(1)} %get-tuple-element.124, pred[]{:T(512)S(6)} %xor.34), kind=kLoop, calls=%fused_computation.2 | loop fusion | flops 262144 | bytes 2097153 | tf_op jit(solution)/shard_map/jit(_where)/select_n | solution.py:148
  118.9 3.7 %collective-permute-start.46 = (f32[128,1024]{1,0:T(8,128)}, f32[128,1024]{1,0:T(8,128)S(1)}, u32[]{:S(2)}, u32[]{:S(2)}) collective-permute-start(f32[128,1024]{1,0:T(8,128)} %get-tuple-element.128), channel_id=1, source_target_pairs={{0,1},{1,0},{2,3},{3,2},{4,5},{5,4},{6,7},{7,6},{8,9},{9,8},{10,11... | collective-permute-start | bytes 1572872 | tf_op jit(solution)/shard_map/ppermute | solution.py:106
  122.7 0.0 collective-permute-done.47.refs_1_
  122.7 0.0 copy-start.2
  122.7 0.0 copy-done
  122.7 0.7 copy-done.2
  123.4 4.7 %shard_map.37.refs_1_ = f32[256,1024]{1,0:T(8,128)S(1)} custom-call(s32[1]{0:T(128)} %bitcast.own_id, s32[2]{0:T(128)S(1)} %copy-done.1, s32[4,128]{1,0:T(4,128)S(1)} %bitcast.11, f32[256,1024]{1,0:T(8,128)S(1)} %copy-done, f32[256,1024]{1,0:T(8,128)S(1)} %copy-done, f32[128,1024]{1,0:T(8,128)S(1)} %collective-permute-done.47.refs_1_, ...), custom_call_target="tpu_custom_call" | custom-call | flops 2415919104 | bytes 6291456 | tf_op jit(solution)/shard_map/pallas_call | solution.py:86
  128.0 0.0 collective-permute-done.46.refs_0_
  128.0 3.3 %shard_map.38 = f32[256,1024]{1,0:T(8,128)} custom-call(s32[1]{0:T(128)} %bitcast.own_id, s32[2]{0:T(128)S(1)} %copy-done.1, s32[4,128]{1,0:T(4,128)S(1)} %bitcast.12, f32[256,1024]{1,0:T(8,128)S(1)} %copy-done, f32[128,1024]{1,0:T(8,128)S(1)} %collective-permute-done.46.refs_0_, f32[256,1024]{1,0:T(8,128)S(1)} %shard_map.37.refs_1_), custom_call_target="tpu_custom_call" | custom-call | flops 805306368 | bytes 4194304 | tf_op jit(solution)/shard_map/pallas_call | solution.py:86
  (1 shorter events, 0.0 us)
Async XLA Ops:
  1.3 17.2 %copy-start.1 = (s32[2]{0:T(128)S(1)}, s32[2]{0:T(128)}, u32[]{:S(2)}) copy-start(s32[2]{0:T(128)} %rounds.3) | copy-start | bytes 28
  1.3 48.3 %collective-permute-start.45 = (f32[128,1024]{1,0:T(8,128)S(1)}, f32[128,1024]{1,0:T(8,128)}, u32[]{:S(2)}, u32[]{:S(2)}) collective-permute-start(f32[128,1024]{1,0:T(8,128)S(1)} %get-tuple-element.131), channel_id=1, source_target_pairs={{0,511},{1,510},{2,509},{3,508},{4,507},{5,506},{6,505},{7,504},{8... | collective-permute-start | bytes 1572872 | tf_op jit(solution)/shard_map/ppermute | solution.py:106
  20.4 27.3 %collective-permute-start.6 = (f32[128,1024]{1,0:T(8,128)S(1)}, f32[128,1024]{1,0:T(8,128)}, u32[]{:S(2)}, u32[]{:S(2)}) collective-permute-start(f32[128,1024]{1,0:T(8,128)S(1)} %param.7), channel_id=1, source_target_pairs={{0,400},{1,401},{2,402},{3,403},{4,404},{5,405},{6,406},{7,407},{8... | collective-permute-start | bytes 1572872 | tf_op jit(solution)/shard_map/cond/branch_7_fun/ppermute | solution.py:106
  47.6 75.0 %collective-permute-start.47 = (f32[128,1024]{1,0:T(8,128)S(1)}, f32[128,1024]{1,0:T(8,128)S(1)}, u32[]{:S(2)}, u32[]{:S(2)}) collective-permute-start(f32[128,1024]{1,0:T(8,128)S(1)} %get-tuple-element.126), channel_id=1, source_target_pairs={{0,511},{1,510},{2,509},{3,508},{4,507},{5,506},{6,505},{7,504},{8... | collective-permute-start | bytes 1572872 | tf_op jit(solution)/shard_map/ppermute | solution.py:106
  49.6 30.0 %collective-permute-start.21 = (f32[128,1024]{1,0:T(8,128)}, f32[128,1024]{1,0:T(8,128)}, u32[]{:S(2)}, u32[]{:S(2)}) collective-permute-start(f32[128,1024]{1,0:T(8,128)} %param.23), channel_id=1, source_target_pairs={{0,400},{1,401},{2,402},{3,403},{4,404},{5,405},{6,406},{7,407},{8... | collective-permute-start | bytes 1572872 | tf_op jit(solution)/shard_map/cond/branch_7_fun/ppermute | solution.py:106
  81.0 30.6 %collective-permute-start.37 = (f32[128,1024]{1,0:T(8,128)S(1)}, f32[128,1024]{1,0:T(8,128)S(1)}, u32[]{:S(2)}, u32[]{:S(2)}) collective-permute-start(f32[128,1024]{1,0:T(8,128)S(1)} %get-tuple-element.111), channel_id=1, source_target_pairs={{0,112},{1,113},{2,114},{3,115},{4,116},{5,117},{6,118},{7,119},{8... | collective-permute-start | bytes 1572872 | tf_op jit(solution)/shard_map/cond/branch_4_fun/ppermute | solution.py:106
  87.9 29.0 %collective-permute-start.38 = (f32[128,1024]{1,0:T(8,128)S(1)}, f32[128,1024]{1,0:T(8,128)}, u32[]{:S(2)}, u32[]{:S(2)}) collective-permute-start(f32[128,1024]{1,0:T(8,128)S(1)} %get-tuple-element.112), channel_id=1, source_target_pairs={{0,398},{1,399},{2,396},{3,397},{4,394},{5,395},{6,392},{7,393},{8... | collective-permute-start | bytes 1572872 | tf_op jit(solution)/shard_map/cond/branch_4_fun/ppermute | solution.py:106
  116.9 5.8 %copy-start = (f32[256,1024]{1,0:T(8,128)S(1)}, f32[256,1024]{1,0:T(8,128)}, u32[]{:S(2)}) copy-start(f32[256,1024]{1,0:T(8,128)} %own.3) | copy-start | bytes 3145732
  118.9 9.1 %collective-permute-start.46 = (f32[128,1024]{1,0:T(8,128)}, f32[128,1024]{1,0:T(8,128)S(1)}, u32[]{:S(2)}, u32[]{:S(2)}) collective-permute-start(f32[128,1024]{1,0:T(8,128)} %get-tuple-element.128), channel_id=1, source_target_pairs={{0,1},{1,0},{2,3},{3,2},{4,5},{5,4},{6,7},{7,6},{8,9},{9,8},{10,11... | collective-permute-start | bytes 1572872 | tf_op jit(solution)/shard_map/ppermute | solution.py:106
  122.7 0.7 copy-start.2
